TPU v7x, 256 devices: a whole 4x4x8 slice. The times are simulated.
256 devices in a mesh: dp: 16 (over z_lo, x, core), seq: 16 (over y, z_hi).
Axes of the slice: x: 4, y: 4, z: 8 (z_hi: 4, z_lo: 2; z = z_hi * 2 + z_lo), core: 2. Of those that a mesh axis runs over, the one named last changes fastest.
Arguments:
- queries: bfloat16 [16, 2048, 1536], P('dp', 'seq'), may hold values from -8 to 8
- keys: bfloat16 [16, 2048, 1536], P('dp', 'seq'), may hold values from -8 to 8
- values: bfloat16 [16, 2048, 1536], P('dp', 'seq'), may hold values from -12 to 12
- residual: bfloat16 [16, 2048, 1536], P('dp', 'seq'), may hold values from -6 to 6
- out_weight: bfloat16 [1536, 1536], P('seq'), may hold values from -0.15625 to 0.15625
- conv_weight: bfloat16 [5, 1536, 384], P(None, 'seq'), may hold values from -0.0625 to 0.0625
- skip: bfloat16 [16, 4096, 384], P('dp', 'seq'), may hold values from -6 to 6
- cotangent: bfloat16 [16, 4096, 384], P('dp', 'seq'), may hold values from -6 to 6
Outputs:
- decoded: bfloat16 [16, 4096, 384], P('dp', 'seq')
- grad_queries: bfloat16 [16, 2048, 1536], P('dp', 'seq')
- grad_keys: bfloat16 [16, 2048, 1536], P('dp', 'seq')
- grad_values: bfloat16 [16, 2048, 1536], P('dp', 'seq')
- grad_residual: bfloat16 [16, 2048, 1536], P('dp', 'seq')
- grad_out_weight: float32 [1536, 1536], P('seq')
- grad_conv_weight: float32 [5, 1536, 384], P(None, 'seq')
All inputs are finite; a program needn't handle non-finite values.
Results may differ from a plain program's by a relative error of at most 0.029.
Values may be sent and summed in bfloat16 or wider, within the bound.
No kernel may reach another device: no remote copies, remote signals or barrier semaphores. Data moves between devices by JAX's collectives and lax.ppermute only.
A program may use at most 128 MiB of HBM per device.

v0:
```python
import math

import jax
import jax.numpy as jnp
from jax import lax
from jax.sharding import PartitionSpec as P

HEADS = 8


root_two_pi = math.sqrt(2.0 / math.pi)
cubic_term = 0.044715


def with_halo(block, sides, width):
    for axis, dim in sides:
        count = lax.axis_size(axis)
        forward = [(i, i + 1) for i in range(count - 1)]
        backward = [(target, source) for source, target in forward]
        low = lax.ppermute(
            lax.slice_in_dim(block, block.shape[dim] - width, None, axis=dim), axis, forward
        )
        high = lax.ppermute(lax.slice_in_dim(block, 0, width, axis=dim), axis, backward)
        block = jnp.concatenate([low, block, high], axis=dim)
    return block


def gelu_pair(pre_act):
    inner_arg = root_two_pi * (pre_act + cubic_term * pre_act * pre_act * pre_act)
    tanh_value = jnp.tanh(inner_arg)
    activated = 0.5 * pre_act * (1.0 + tanh_value)
    act_slope = 0.5 * (1.0 + tanh_value) + 0.5 * pre_act * (
        1.0 - tanh_value * tanh_value
    ) * root_two_pi * (1.0 + 3.0 * cubic_term * pre_act * pre_act)
    return (activated, act_slope)


def attention_forward(head_queries, head_keys, head_values, score_scale):
    scores = (
        lax.dot_general(
            head_queries, head_keys, (((1,), (1,)), ((), ())), preferred_element_type=jnp.float32
        )
        * score_scale
    )
    row_peak = jnp.max(scores, axis=1, keepdims=True)
    shifted_exp = jnp.exp(scores - row_peak)
    attn_probs = shifted_exp / jnp.sum(shifted_exp, axis=1, keepdims=True)
    probs_low = attn_probs.astype(jnp.bfloat16)
    attended = jnp.dot(probs_low, head_values, preferred_element_type=jnp.float32).astype(
        jnp.bfloat16
    )
    return (attn_probs, probs_low, attended)


def attention_backward(
    head_queries, head_keys, head_values, attn_probs, probs_low, grad_out, score_scale
):
    grad_probs = lax.dot_general(
        grad_out, head_values, (((1,), (1,)), ((), ())), preferred_element_type=jnp.float32
    )
    row_total = jnp.sum(attn_probs * grad_probs, axis=1, keepdims=True)
    grad_scores = (attn_probs * (grad_probs - row_total) * score_scale).astype(jnp.bfloat16)
    grad_query = jnp.dot(grad_scores, head_keys, preferred_element_type=jnp.float32).astype(
        jnp.bfloat16
    )
    grad_key = lax.dot_general(
        grad_scores, head_queries, (((0,), (0,)), ((), ())), preferred_element_type=jnp.float32
    )
    grad_value = lax.dot_general(
        probs_low, grad_out, (((0,), (0,)), ((), ())), preferred_element_type=jnp.float32
    )
    return (grad_query, grad_key, grad_value)


def body(queries, keys, values, residual, out_weight, conv_weight, skip, cotangent):
    seq_count = lax.axis_size("seq")
    tok_rows = queries.shape[1]
    model_width = queries.shape[2]
    head_size = model_width // HEADS
    head_split = seq_count // HEADS
    part_rows = tok_rows // head_split
    score_scale = head_size ** (-0.5)
    full_proj, full_conv = (
        lax.all_gather(out_weight, "seq", axis=0, tiled=True),
        lax.all_gather(conv_weight, "seq", axis=1, tiled=True),
    )
    kernel_taps = full_conv.shape[0]
    half_kernel = kernel_taps // 2
    rim_tokens = (half_kernel + 1) // 2
    tap_offset = 2 * rim_tokens - half_kernel
    positions = 2 * tok_rows

    def to_parts(block):
        return (
            block.reshape(head_split, part_rows, HEADS, head_size)
            .transpose(2, 0, 1, 3)
            .reshape(HEADS * head_split, part_rows, head_size)
        )

    def from_parts(block):
        return (
            block.reshape(HEADS, head_split, part_rows, head_size)
            .transpose(1, 2, 0, 3)
            .reshape(tok_rows, model_width)
        )

    def repeated(block):
        return jnp.repeat(
            block.reshape(tok_rows, HEADS, head_size).transpose(1, 0, 2), head_split, axis=0
        )

    def summed_parts(block):
        return (
            block.reshape(HEADS, head_split, tok_rows, head_size)
            .sum(axis=1)
            .transpose(1, 0, 2)
            .reshape(tok_rows, model_width)
            .astype(jnp.bfloat16)
        )

    query_flat = queries[0]
    key_flat = keys[0]
    value_flat = values[0]
    part_q, part_k, part_v = (
        lax.all_to_all(to_parts(query_flat), "seq", split_axis=0, concat_axis=0, tiled=True),
        lax.all_to_all(repeated(key_flat), "seq", split_axis=0, concat_axis=0, tiled=True),
        lax.all_to_all(repeated(value_flat), "seq", split_axis=0, concat_axis=0, tiled=True),
    )
    head_keys = part_k.reshape(-1, head_size)
    head_values = part_v.reshape(-1, head_size)
    head_queries = part_q.reshape(-1, head_size)
    attn_probs, probs_low, attended = attention_forward(
        head_queries, head_keys, head_values, score_scale
    )
    back_parts = lax.all_to_all(
        attended.reshape(seq_count, part_rows, head_size),
        "seq",
        split_axis=0,
        concat_axis=0,
        tiled=True,
    )
    attended_rows = from_parts(back_parts)
    mixed = (
        residual[0].astype(jnp.float32)
        + jnp.dot(attended_rows, full_proj, preferred_element_type=jnp.float32)
    ).astype(jnp.bfloat16)
    mixed_pad = with_halo(mixed[None], (("seq", 1),), rim_tokens)[0]
    upsampled = jnp.repeat(mixed_pad, 2, axis=0)
    stacked_in = jnp.stack(
        [
            upsampled[tap_offset + tap_index : tap_offset + tap_index + positions]
            for tap_index in range(kernel_taps)
        ],
        axis=1,
    )
    pre_act = lax.dot_general(
        stacked_in, full_conv, (((1, 2), (0, 1)), ((), ())), preferred_element_type=jnp.float32
    )
    activated, act_slope = gelu_pair(pre_act)
    decoded = (activated + skip[0].astype(jnp.float32)).astype(jnp.bfloat16)
    grad_pre = (cotangent[0].astype(jnp.float32) * act_slope).astype(jnp.bfloat16)
    grad_pad = with_halo(grad_pre[None], (("seq", 1),), half_kernel)[0]
    stacked_grad = jnp.stack(
        [
            grad_pad[2 * half_kernel - tap_index : 2 * half_kernel - tap_index + positions]
            for tap_index in range(kernel_taps)
        ],
        axis=1,
    )
    grad_up = lax.dot_general(
        stacked_grad, full_conv, (((1, 2), (0, 2)), ((), ())), preferred_element_type=jnp.float32
    )
    grad_mixed = grad_up.reshape(tok_rows, 2, model_width).sum(axis=1).astype(jnp.bfloat16)
    grad_attended = lax.dot_general(
        grad_mixed, full_proj, (((1,), (1,)), ((), ())), preferred_element_type=jnp.float32
    ).astype(jnp.bfloat16)
    head_grad = lax.all_to_all(
        to_parts(grad_attended), "seq", split_axis=0, concat_axis=0, tiled=True
    ).reshape(-1, head_size)
    grad_query, grad_key, grad_value = attention_backward(
        head_queries, head_keys, head_values, attn_probs, probs_low, head_grad, score_scale
    )
    back_q = lax.all_to_all(
        grad_query.reshape(seq_count, part_rows, head_size),
        "seq",
        split_axis=0,
        concat_axis=0,
        tiled=True,
    )
    out_queries = from_parts(back_q)
    back_k, back_v = (
        lax.all_to_all(
            grad_key.reshape(seq_count, tok_rows, head_size).astype(jnp.bfloat16),
            "seq",
            split_axis=0,
            concat_axis=0,
            tiled=True,
        ).astype(jnp.float32),
        lax.all_to_all(
            grad_value.reshape(seq_count, tok_rows, head_size).astype(jnp.bfloat16),
            "seq",
            split_axis=0,
            concat_axis=0,
            tiled=True,
        ).astype(jnp.float32),
    )
    out_keys = summed_parts(back_k)
    out_values = summed_parts(back_v)
    proj_term = lax.dot_general(
        attended_rows, grad_mixed, (((0,), (0,)), ((), ())), preferred_element_type=jnp.float32
    ).astype(jnp.bfloat16)
    conv_term = jnp.stack(
        [
            lax.dot_general(
                upsampled[tap_offset + tap_index : tap_offset + tap_index + positions],
                grad_pre,
                (((0,), (0,)), ((), ())),
                preferred_element_type=jnp.float32,
            ).astype(jnp.bfloat16)
            for tap_index in range(kernel_taps)
        ]
    )
    proj_shard, conv_shard = (
        lax.psum_scatter(proj_term, "seq", scatter_dimension=0, tiled=True).astype(jnp.float32),
        lax.psum_scatter(conv_term, "seq", scatter_dimension=1, tiled=True).astype(jnp.float32),
    )
    proj_total, conv_total = (
        lax.psum(proj_shard.astype(jnp.bfloat16), "dp").astype(jnp.float32),
        lax.psum(conv_shard.astype(jnp.bfloat16), "dp").astype(jnp.float32),
    )
    return (
        decoded[None],
        out_queries[None],
        out_keys[None],
        out_values[None],
        grad_mixed[None],
        proj_total,
        conv_total,
    )


def solution(mesh):
    in_specs = (
        P("dp", "seq", None),
        P("dp", "seq", None),
        P("dp", "seq", None),
        P("dp", "seq", None),
        P("seq", None),
        P(None, "seq", None),
        P("dp", "seq", None),
        P("dp", "seq", None),
    )
    out_specs = (
        P("dp", "seq", None),
        P("dp", "seq", None),
        P("dp", "seq", None),
        P("dp", "seq", None),
        P("dp", "seq", None),
        P("seq", None),
        P(None, "seq", None),
    )
    return jax.shard_map(body, mesh=mesh, in_specs=in_specs, out_specs=out_specs, check_vma=False)
```

profile of v0, /device:TPU:1, one launch (start us, length us, event | category | flops | bytes accessed | tf_op | source)
XLA Modules:
  0.0 627.4 jit_solution(17845061077027830002)
XLA Ops:
  8.7 1.4 reshape_squeeze.9
  11.0 11.7 %all-to-all-start = ((bf16[16,64,192]{2,1,0:T(8,128)(2,1)}), bf16[16,64,192]{2,1,0:T(8,128)(2,1)S(1)}, u32[]{:S(2)}, u32[]{:S(2)}) async-start(bf16[16,64,192]{2,1,0:T(8,128)(2,1)} %bitcast.2), calls=%async_computation | async-start | bytes 1048576 | tf_op jit(solution)/shard_map/all_to_all | solution.py:125
  22.8 1.2 copy.52
  24.0 18.4 %all-to-all-done = bf16[16,64,192]{2,1,0:T(8,128)(2,1)S(1)} async-done(((bf16[16,64,192]{2,1,0:T(8,128)(2,1)}), bf16[16,64,192]{2,1,0:T(8,128)(2,1)S(1)}, u32[]{:S(2)}, u32[]{:S(2)}) %all-to-all-start) | async-done | bytes 393248 | tf_op jit(solution)/shard_map/all_to_all | solution.py:125
  43.5 4.7 all-to-all-start.1
  48.4 14.6 %all-to-all-done.1 = bf16[16,128,192]{1,2,0:T(8,128)(2,1)S(1)} async-done(((bf16[16,128,192]{1,2,0:T(8,128)(2,1)}), bf16[16,128,192]{1,2,0:T(8,128)(2,1)S(1)}, u32[]{:S(2)}, u32[]{:S(2)}) %all-to-all-start.1) | async-done | bytes 786464 | tf_op jit(solution)/shard_map/all_to_all | solution.py:126
  63.0 1.2 broadcast_in_dim.31
  64.2 4.6 all-to-all-start.2
  68.8 1.3 multiply_reduce_fusion.1
  70.1 1.9 fusion.1
  72.1 6.0 convert_bitcast_fusion
  78.1 18.6 %all-to-all-done.2 = bf16[16,128,192]{1,2,0:T(8,128)(2,1)S(1)} async-done(((bf16[16,128,192]{1,2,0:T(8,128)(2,1)}), bf16[16,128,192]{1,2,0:T(8,128)(2,1)S(1)}, u32[]{:S(2)}, u32[]{:S(2)}) %all-to-all-start.2) | async-done | bytes 786464 | tf_op jit(solution)/shard_map/all_to_all | solution.py:127
  96.7 5.0 fusion.15
  101.9 30.7 %all_to_all.40 = bf16[16,64,192]{2,1,0:T(8,128)(2,1)S(1)} all-to-all(bf16[16,64,192]{2,1,0:T(8,128)(2,1)S(1)} %bitcast.190), channel_id=1, replica_groups=mesh['dp'=16,'seq'=16] {'seq'}, dimensions={0} | all-to-all | bytes 786432 | tf_op jit(solution)/shard_map/all_to_all | solution.py:135
  133.3 3.1 fusion.12
  136.5 1.3 collective-permute-start.1
  137.8 5.3 collective-permute-start
  143.5 1.2 stack.56
  146.1 1.2 stack.54
  147.3 1.3 broadcast_in_dim.34
  148.7 3.0 reshape.149
  151.7 1.4 broadcast_in_dim.36
  153.1 1.2 stack.58
  154.3 2.2 constant_dynamic-update-slice_fusion.2
  156.5 2.2 bitcast_dynamic-update-slice_fusion.1
  158.7 2.1 constant_dynamic-update-slice_fusion.1
  160.8 1.1 bitcast_dynamic-update-slice_fusion
  162.8 54.5 %all-gather.5.cloned.1.call-done = bf16[5,1536,384]{2,1,0:T(8,128)(2,1)} async-done(((bf16[5,96,384]{2,1,0:T(8,128)(2,1)}), bf16[5,1536,384]{2,1,0:T(8,128)(2,1)}) %all-gather.5.cloned.1.call-update) | async-done | bytes 5898256 | tf_op jit(solution)/shard_map/all_gather | solution.py:85
  217.3 7.1 %fusion.36 = (bf16[256,384]{1,0:T(8,128)(2,1)S(1)}, bf16[1,256,384]{2,1,0:T(8,128)(2,1)}) fusion(bf16[1,256,384]{2,1,0:T(8,128)(2,1)} %param.15, bf16[1,256,384]{2,1,0:T(8,128)(2,1)} %param.14, bf16[256,5,1536]{2,0,1:T(8,128)(2,1)} %constant_dynamic-update-slice_fusion, bf16[5,1536,384]{2,1,0:T(8,128)(2,1)} %all-gather.5.cloned.1.call-done), kind=kOutput, calls=%fused_computation.60 | convolution fusion | flops 1512308736 | bytes 10616832 | tf_op jit(solution)/shard_map/dot_general | solution.py:156
  224.4 1.3 collective-permute-start.2
  225.7 12.8 %collective-permute-start.3 = (bf16[1,2,384]{2,1,0:T(2,128)(2,1)S(1)}, bf16[1,2,384]{2,1,0:T(2,128)(2,1)S(1)}, u32[]{:S(2)}, u32[]{:S(2)}) collective-permute-start(bf16[1,2,384]{2,1,0:T(2,128)(2,1)S(1)} %get-tuple-element.38), channel_id=1, source_target_pairs={{0,1},{1,2},{2,3},{3,4},{4,5},{5,6},{6,7},{7,8},{8,9},{9,10},{10,1... | collective-permute-start | bytes 4616 | tf_op jit(solution)/shard_map/ppermute | solution.py:20
  239.2 3.0 convolution_bitcast_fusion
  242.1 3.1 reshape.150
  245.2 4.1 reduce_sum.46
  249.3 4.6 convolution_convert_fusion
  253.9 1.2 slice.88
  255.1 1.2 slice.87
  256.3 1.2 slice.89
  257.5 2.9 fusion.3
  260.3 2.8 fusion.5
  263.2 1.6 fusion.7
  264.8 1.7 fusion.9
  266.5 1.6 fusion.11
  268.1 4.1 convolution_convert_fusion.6
  272.7 32.5 %all_to_all.41 = bf16[16,64,192]{2,1,0:T(8,128)(2,1)S(1)} all-to-all(bf16[16,64,192]{2,1,0:T(8,128)(2,1)S(1)} %bitcast.195), channel_id=1, replica_groups=mesh['dp'=16,'seq'=16] {'seq'}, dimensions={0} | all-to-all | bytes 786432 | tf_op jit(solution)/shard_map/all_to_all | solution.py:177
  305.2 4.9 multiply_reduce_fusion
  310.2 1.1 slice-done.1
  311.3 1.4 multiply_convert_fusion
  312.6 2.0 copy-done
  314.6 1.5 convolution_convert_fusion.9
  317.2 6.7 %all-to-all-start.5 = ((bf16[16,64,192]{2,1,0:T(8,128)(2,1)}), bf16[16,64,192]{2,1,0:T(8,128)(2,1)S(1)}, u32[]{:S(2)}, u32[]{:S(2)}) async-start(bf16[16,64,192]{2,1,0:T(8,128)(2,1)} %bitcast.33), calls=%async_computation.5 | async-start | bytes 1048576 | tf_op jit(solution)/shard_map/all_to_all | solution.py:183
  323.8 6.4 %copy.69 = bf16[2048,1024]{1,0:T(8,128)(2,1)} copy(bf16[2048,1024]{0,1:T(8,128)(2,1)} %bitcast.176) | data formatting | bytes 8388608 | tf_op jit(solution)/shard_map/dot_general | solution.py:66
  330.2 4.6 convolution_convert_fusion.8
  334.9 8.8 %all-to-all-done.5 = bf16[16,64,192]{2,1,0:T(8,128)(2,1)S(1)} async-done(((bf16[16,64,192]{2,1,0:T(8,128)(2,1)}), bf16[16,64,192]{2,1,0:T(8,128)(2,1)S(1)}, u32[]{:S(2)}, u32[]{:S(2)}) %all-to-all-start.5) | async-done | bytes 393248 | tf_op jit(solution)/shard_map/all_to_all | solution.py:183
  343.7 7.1 %all-to-all-start.6 = ((bf16[16,128,192]{1,2,0:T(8,128)(2,1)}), bf16[16,128,192]{1,2,0:T(8,128)(2,1)S(1)}, u32[]{:S(2)}, u32[]{:S(2)}) async-start(bf16[16,128,192]{1,2,0:T(8,128)(2,1)} %convolution_convert_fusion.8), calls=%async_computation.6 | async-start | bytes 1572864 | tf_op jit(solution)/shard_map/all_to_all | solution.py:192
  350.8 6.4 %copy.71 = bf16[2048,1024]{1,0:T(8,128)(2,1)} copy(bf16[2048,1024]{0,1:T(8,128)(2,1)} %get-tuple-element.30) | data formatting | bytes 8388608 | tf_op jit(solution)/shard_map/dot_general | solution.py:69
  357.2 4.7 convolution_convert_fusion.7
  361.9 16.1 %all-to-all-done.6 = bf16[16,128,192]{1,2,0:T(8,128)(2,1)S(1)} async-done(((bf16[16,128,192]{1,2,0:T(8,128)(2,1)}), bf16[16,128,192]{1,2,0:T(8,128)(2,1)S(1)}, u32[]{:S(2)}, u32[]{:S(2)}) %all-to-all-start.6) | async-done | bytes 786464 | tf_op jit(solution)/shard_map/all_to_all | solution.py:192
  377.9 8.8 %all-to-all-start.7 = ((bf16[16,128,192]{1,2,0:T(8,128)(2,1)}), bf16[16,128,192]{1,2,0:T(8,128)(2,1)S(1)}, u32[]{:S(2)}, u32[]{:S(2)}) async-start(bf16[16,128,192]{1,2,0:T(8,128)(2,1)} %convolution_convert_fusion.7), calls=%async_computation.7 | async-start | bytes 1572864 | tf_op jit(solution)/shard_map/all_to_all | solution.py:199
  386.8 108.0 %reduce-scatter.5.cloned.1.call-done = bf16[5,96,384]{2,1,0:T(8,128)(2,1)} async-done(((bf16[5,1536,384]{2,1,0:T(8,128)(2,1)}), bf16[5,96,384]{2,1,0:T(8,128)(2,1)}) %reduce-scatter.5.cloned.1.call-update) | async-done | bytes 368656 | tf_op jit(solution)/shard_map/reduce_scatter | solution.py:225
  495.1 1.2 broadcast_in_dim_reshape.3
  498.4 118.5 %all-reduce.3.cloned.1.call-done = (bf16[96,1536]{1,0:T(8,128)(2,1)}, bf16[5,96,384]{2,1,0:T(8,128)(2,1)}) async-done(((bf16[96,1536]{1,0:T(8,128)(2,1)}, bf16[5,96,384]{2,1,0:T(8,128)(2,1)}), (bf16[96,1536]{1,0:T(8,128)(2,1)}, bf16[5,96,384]{2,1,0:T(8,128)(2,1)})) %all-reduce.3.cloned.1.call-update) | async-done | bytes 663568 | tf_op jit(solution)/shard_map/psum | solution.py:228
  616.9 1.8 convert_element_type.156
  618.8 1.9 convert_element_type.162
  (78 shorter events, 12.2 us)
Async XLA Ops:
  7.2 41.0 %copy-start.14 = (bf16[1,128,1536]{2,1,0:T(8,128)(2,1)S(1)}, bf16[1,128,1536]{2,1,0:T(8,128)(2,1)}, u32[]{:S(2)}) copy-start(bf16[1,128,1536]{2,1,0:T(8,128)(2,1)} %param.10) | copy-start | bytes 1179652
  7.2 126.1 %all-gather.3.cloned.1.call-start = ((), (), s32[]{:S(2)}) async-start(), calls=%async_computation.10 | async-start | bytes 5013504 | tf_op jit(solution)/shard_map/all_gather | solution.py:84
  7.9 209.4 %all-gather.5.cloned.1.call-start = ((), (), s32[]{:S(2)}) async-start(), calls=%async_computation.11 | async-start | bytes 6266880 | tf_op jit(solution)/shard_map/all_gather | solution.py:85
  11.0 31.4 %all-to-all-start = ((bf16[16,64,192]{2,1,0:T(8,128)(2,1)}), bf16[16,64,192]{2,1,0:T(8,128)(2,1)S(1)}, u32[]{:S(2)}, u32[]{:S(2)}) async-start(bf16[16,64,192]{2,1,0:T(8,128)(2,1)} %bitcast.2), calls=%async_computation | async-start | bytes 1048576 | tf_op jit(solution)/shard_map/all_to_all | solution.py:125
  42.4 27.7 %copy-start.3 = (bf16[16,64,192]{2,1,0:T(8,128)(2,1)}, bf16[16,64,192]{2,1,0:T(8,128)(2,1)S(1)}, u32[]{:S(2)}) copy-start(bf16[16,64,192]{2,1,0:T(8,128)(2,1)S(1)} %all-to-all-done) | copy-start | bytes 1179652
  43.5 19.5 %all-to-all-start.1 = ((bf16[16,128,192]{1,2,0:T(8,128)(2,1)}), bf16[16,128,192]{1,2,0:T(8,128)(2,1)S(1)}, u32[]{:S(2)}, u32[]{:S(2)}) async-start(bf16[16,128,192]{1,2,0:T(8,128)(2,1)} %bitcast.6), calls=%async_computation.1 | async-start | bytes 1572864 | tf_op jit(solution)/shard_map/all_to_all | solution.py:126
  63.0 7.2 %copy-start.9 = (bf16[16,128,192]{1,2,0:T(8,128)(2,1)}, bf16[16,128,192]{1,2,0:T(8,128)(2,1)S(1)}, u32[]{:S(2)}) copy-start(bf16[16,128,192]{1,2,0:T(8,128)(2,1)S(1)} %all-to-all-done.1) | copy-start | bytes 2359300
  64.2 32.5 %all-to-all-start.2 = ((bf16[16,128,192]{1,2,0:T(8,128)(2,1)}), bf16[16,128,192]{1,2,0:T(8,128)(2,1)S(1)}, u32[]{:S(2)}, u32[]{:S(2)}) async-start(bf16[16,128,192]{1,2,0:T(8,128)(2,1)} %bitcast.9), calls=%async_computation.2 | async-start | bytes 1572864 | tf_op jit(solution)/shard_map/all_to_all | solution.py:127
  68.7 318.1 %reduce-scatter.3.cloned.1.call-start = ((), (), s32[]{:S(2)}) async-start(), calls=%async_computation.12 | async-start | bytes 5013504 | tf_op jit(solution)/shard_map/reduce_scatter | solution.py:224
  96.7 36.6 %copy-start.13 = (bf16[1,128,1536]{2,1,0:T(8,128)(2,1)S(1)}, bf16[1,128,1536]{2,1,0:T(8,128)(2,1)}, u32[]{:S(2)}) copy-start(bf16[1,128,1536]{2,1,0:T(8,128)(2,1)} %param.11) | copy-start | bytes 1179652
  136.5 8.3 %collective-permute-start.1 = (bf16[1,1,1536]{2,1,0:T(2,128)(2,1)S(1)}, bf16[1,1,1536]{2,1,0:T(2,128)(2,1)S(1)}, u32[]{:S(2)}, u32[]{:S(2)}) collective-permute-start(bf16[1,1,1536]{2,1,0:T(2,128)(2,1)S(1)} %get-tuple-element.36), channel_id=1, source_target_pairs={{1,0},{2,1},{3,2},{4,3},{5,4},{6,5},{7,6},{8,7},{9,8},{10,9},{11,1... | collective-permute-start | bytes 9224 | tf_op jit(solution)/shard_map/ppermute | solution.py:23
  137.8 7.0 %collective-permute-start = (bf16[1,1,1536]{2,1,0:T(2,128)(2,1)S(1)}, bf16[1,1,1536]{2,1,0:T(2,128)(2,1)S(1)}, u32[]{:S(2)}, u32[]{:S(2)}) collective-permute-start(bf16[1,1,1536]{2,1,0:T(2,128)(2,1)S(1)} %get-tuple-element.37), channel_id=1, source_target_pairs={{0,1},{1,2},{2,3},{3,4},{4,5},{5,6},{6,7},{7,8},{8,9},{9,10},{10,1... | collective-permute-start | bytes 9224 | tf_op jit(solution)/shard_map/ppermute | solution.py:20
  154.3 6.5 %copy-start.1 = (bf16[260,1536]{1,0:T(8,128)(2,1)S(1)}, bf16[260,1536]{1,0:T(8,128)(2,1)}, u32[]{:S(2)}) copy-start(bf16[260,1536]{1,0:T(8,128)(2,1)} %reshape.149) | copy-start | bytes 2396164
  154.3 7.6 %copy-start.8 = (bf16[256,1,1536]{2,0,1:T(8,128)(2,1)S(1)}, bf16[256,1,1536]{2,0,1:T(8,128)(2,1)}, u32[]{:S(2)}) copy-start(bf16[256,1,1536]{2,0,1:T(8,128)(2,1)} %stack.58) | copy-start | bytes 2359300
  217.3 21.9 %copy-start.15 = (bf16[5,1536,384]{2,1,0:T(8,128)(2,1)S(1)}, bf16[5,1536,384]{2,1,0:T(8,128)(2,1)}, u32[]{:S(2)}) copy-start(bf16[5,1536,384]{2,1,0:T(8,128)(2,1)} %all-gather.5.cloned.1.call-done) | copy-start | bytes 17694724
  224.4 14.7 %copy-start.5 = (bf16[256,384]{1,0:T(8,128)(2,1)}, bf16[256,384]{1,0:T(8,128)(2,1)S(1)}, u32[]{:S(2)}) copy-start(bf16[256,384]{1,0:T(8,128)(2,1)S(1)} %get-tuple-element.32) | copy-start | bytes 589828
  224.4 14.1 %collective-permute-start.2 = (bf16[1,2,384]{2,1,0:T(2,128)(2,1)S(1)}, bf16[1,2,384]{2,1,0:T(2,128)(2,1)S(1)}, u32[]{:S(2)}, u32[]{:S(2)}) collective-permute-start(bf16[1,2,384]{2,1,0:T(2,128)(2,1)S(1)} %get-tuple-element.39), channel_id=1, source_target_pairs={{1,0},{2,1},{3,2},{4,3},{5,4},{6,5},{7,6},{8,7},{9,8},{10,9},{11,1... | collective-permute-start | bytes 4616 | tf_op jit(solution)/shard_map/ppermute | solution.py:23
  225.7 13.3 %collective-permute-start.3 = (bf16[1,2,384]{2,1,0:T(2,128)(2,1)S(1)}, bf16[1,2,384]{2,1,0:T(2,128)(2,1)S(1)}, u32[]{:S(2)}, u32[]{:S(2)}) collective-permute-start(bf16[1,2,384]{2,1,0:T(2,128)(2,1)S(1)} %get-tuple-element.38), channel_id=1, source_target_pairs={{0,1},{1,2},{2,3},{3,4},{4,5},{5,6},{6,7},{7,8},{8,9},{9,10},{10,1... | collective-permute-start | bytes 4616 | tf_op jit(solution)/shard_map/ppermute | solution.py:20
  253.8 3.6 copy-start.6
  253.9 240.9 %reduce-scatter.5.cloned.1.call-start = ((), (), s32[]{:S(2)}) async-start(), calls=%async_computation.13 | async-start | bytes 6266880 | tf_op jit(solution)/shard_map/reduce_scatter | solution.py:225
  256.3 8.5 %copy-start.2 = (bf16[260,1536]{1,0:T(8,128)(2,1)S(1)}, bf16[260,1536]{1,0:T(8,128)(2,1)}, u32[]{:S(2)}) copy-start(bf16[260,1536]{1,0:T(8,128)(2,1)} %reshape.149) | copy-start | bytes 2396164
  257.5 5.7 copy-start.12
  260.3 6.1 copy-start.11
  266.5 1.7 copy-start.7
  305.2 4.9 slice-start
  305.2 6.0 slice-start.1
  311.3 3.4 copy-start.10
  312.6 2.0 copy-start
  317.1 13.1 %copy-start.4 = (bf16[16,64,192]{2,1,0:T(8,128)(2,1)S(1)}, bf16[16,64,192]{2,1,0:T(8,128)(2,1)}, u32[]{:S(2)}) copy-start(bf16[16,64,192]{2,1,0:T(8,128)(2,1)} %copy-done.3) | copy-start | bytes 1179652
  317.2 26.5 %all-to-all-start.5 = ((bf16[16,64,192]{2,1,0:T(8,128)(2,1)}), bf16[16,64,192]{2,1,0:T(8,128)(2,1)S(1)}, u32[]{:S(2)}, u32[]{:S(2)}) async-start(bf16[16,64,192]{2,1,0:T(8,128)(2,1)} %bitcast.33), calls=%async_computation.5 | async-start | bytes 1048576 | tf_op jit(solution)/shard_map/all_to_all | solution.py:183
  343.7 34.3 %all-to-all-start.6 = ((bf16[16,128,192]{1,2,0:T(8,128)(2,1)}), bf16[16,128,192]{1,2,0:T(8,128)(2,1)S(1)}, u32[]{:S(2)}, u32[]{:S(2)}) async-start(bf16[16,128,192]{1,2,0:T(8,128)(2,1)} %convolution_convert_fusion.8), calls=%async_computation.6 | async-start | bytes 1572864 | tf_op jit(solution)/shard_map/all_to_all | solution.py:192
  377.9 119.4 %all-to-all-start.7 = ((bf16[16,128,192]{1,2,0:T(8,128)(2,1)}), bf16[16,128,192]{1,2,0:T(8,128)(2,1)S(1)}, u32[]{:S(2)}, u32[]{:S(2)}) async-start(bf16[16,128,192]{1,2,0:T(8,128)(2,1)} %convolution_convert_fusion.7), calls=%async_computation.7 | async-start | bytes 1572864 | tf_op jit(solution)/shard_map/all_to_all | solution.py:199
  386.7 230.2 %all-reduce.3.cloned.1.call-start = ((), (), s32[]{:S(2)}) async-start(), calls=%async_computation.14 | async-start | bytes 1327104 | tf_op jit(solution)/shard_map/psum | solution.py:228
Sparse Core Ops, SparseCore 0:
  10.5 91.9 all-gather.2
  104.9 112.3 all-gather.4
  254.0 130.0 reduce-scatter.2
  387.6 107.1 reduce-scatter.4
  497.4 119.5 all-reduce.2
where the time goes:
time: 638 us; the launch traced here: 627 us
  waiting for transfers between devices  359 us (56%)
  starting transfers between devices  64.4 us (10%)
  blocking collectives  63.2 us (10%)
  matrix products  54.5 us (9%)
  local copies, waits for them, and re-layouts  53 us (8%)
  other arithmetic  18.7 us (3%)
  between operations  14.4 us (2%)
    psum x1, waiting for transfers between devices, body(): lax.psum(proj_shard.astype(jnp.bfloat16), 'dp').astype(jnp.float32)  119 us
    reduce_scatter x1, waiting for transfers between devices, body(): lax.psum_scatter(conv_term, 'seq', scatter_dimension=1, tiled=True)  108 us
    all_gather x1, waiting for transfers between devices, body(): lax.all_gather(conv_weight, 'seq', axis=1, tiled=True)  54.5 us
    all_to_all x1, blocking collectives, body(): lax.all_to_all(to_parts(grad_attended), 'seq', split_axis=0, concat_axis=...  32.5 us
    all_to_all x1, blocking collectives, body(): lax.all_to_all(attended.reshape(seq_count, part_rows, head_size), 'seq',...  30.7 us
    all_to_all x1, waiting for transfers between devices, body(): lax.all_to_all(repeated(value_flat), 'seq', split_axis=0, concat_axis=0,...  18.6 us
    all_to_all x1, waiting for transfers between devices, body(): lax.all_to_all(to_parts(query_flat), 'seq', split_axis=0, concat_axis=0,...  18.4 us
    ppermute x2, starting transfers between devices, with_halo(): lax.ppermute(lax.slice_in_dim(block, block.shape[dim] - width, None, axis...  18.1 us
  transfers between devices with their start and end apart: 15, of which 9 were waited for; matrix products, arithmetic and copies ran while one was open for 16% of the time, Pallas kernels for 0%

commit v1 on v0

v1 whole, which is shorter than its diff:
```python
import math

import jax
import jax.numpy as jnp
from jax import lax
from jax.experimental import pallas as pl
from jax.experimental.pallas import tpu as pltpu
from jax.sharding import Mesh
from jax.sharding import PartitionSpec as P

HEADS = 8
HEAD = 192
WIDTH = 1536
TOK = 128
HALF = 64
CH = 384
TAPS = 5
WCOLS = 768
CCOLS = 1024
TILE = 256
SEQ = ("y", "zh")
ROOT = math.sqrt(2.0 / math.pi)
CUBIC = 0.044715
SCALE = HEAD ** (-0.5)
SCALE2 = SCALE * math.log2(math.e)
BF = jnp.bfloat16
F32 = jnp.float32
VMEM = pl.BlockSpec(memory_space=pltpu.VMEM)
SMEM = pl.BlockSpec(memory_space=pltpu.SMEM)


def params():
    return pltpu.CompilerParams(vmem_limit_bytes=56 * 1024 * 1024)


def cost(flops, nbytes):
    return pl.CostEstimate(flops=int(flops), bytes_accessed=int(nbytes), transcendentals=0)


def shaped(shape, dtype=BF):
    return jax.ShapeDtypeStruct(shape, dtype)


def dot(a, b):
    return jnp.dot(a, b, preferred_element_type=F32)


def dot_nt(a, b):
    return lax.dot_general(a, b, (((1,), (1,)), ((), ())), preferred_element_type=F32)


def pack_kernel(q_ref, k_ref, v_ref, o_ref):
    for j, ref in enumerate((q_ref, k_ref, v_ref)):
        for half in range(2):
            for h in range(HEADS):
                o_ref[half, h, j] = ref[half * HALF : (half + 1) * HALF, h * HEAD : (h + 1) * HEAD]


def pack(q, k, v):
    return pl.pallas_call(
        pack_kernel,
        out_shape=shaped((2, HEADS, 3, HALF, HEAD)),
        in_specs=[VMEM] * 3,
        out_specs=VMEM,
        compiler_params=params(),
        cost_estimate=cost(0, 3 * 2 * TOK * WIDTH * 2),
    )(q, k, v)


def unpack_kernel(x_ref, q_ref, k_ref, v_ref):
    for j, ref in enumerate((q_ref, k_ref, v_ref)):
        for half in range(2):
            for h in range(HEADS):
                ref[half * HALF : (half + 1) * HALF, h * HEAD : (h + 1) * HEAD] = x_ref[half, h, j]


def unpack(x):
    return pl.pallas_call(
        unpack_kernel,
        out_shape=[shaped((TOK, WIDTH))] * 3,
        in_specs=[VMEM],
        out_specs=[VMEM] * 3,
        compiler_params=params(),
        cost_estimate=cost(0, 3 * 2 * TOK * WIDTH * 2),
    )(x)


def rows_of(ref, j):
    return ref[:, j].reshape(16 * HALF, HEAD)


def forward_kernel(mine_ref, other_ref, out_ref, lse_ref, vt_ref):
    step = pl.program_id(0)
    count = 16 * HALF

    @pl.when(step == 0)
    def _():
        vt_ref[:, :count] = rows_of(mine_ref, 2).T
        vt_ref[:, count:] = rows_of(other_ref, 2).T

    q = mine_ref[pl.ds(step * (TILE // HALF), TILE // HALF), 0].reshape(TILE, HEAD)
    s_a = dot_nt(rows_of(mine_ref, 1), q) * SCALE2
    s_b = dot_nt(rows_of(other_ref, 1), q) * SCALE2
    peak = jnp.maximum(jnp.max(s_a, axis=0, keepdims=True), jnp.max(s_b, axis=0, keepdims=True))
    e_a = jnp.exp2(s_a - peak)
    e_b = jnp.exp2(s_b - peak)
    total = jnp.sum(e_a, axis=0, keepdims=True) + jnp.sum(e_b, axis=0, keepdims=True)
    out = dot(vt_ref[:, :count], e_a.astype(BF)) + dot(vt_ref[:, count:], e_b.astype(BF))
    out = (out / total).T.astype(BF)
    out_ref[...] = out.reshape(TILE // HALF, HALF, HEAD)
    lse_ref[...] = peak + jnp.log2(total)


def attention_forward(mine, other):
    whole = pl.BlockSpec((16, 3, HALF, HEAD), lambda i: (0, 0, 0, 0))
    return pl.pallas_call(
        forward_kernel,
        grid=(16 * HALF // TILE,),
        out_shape=[shaped((16, HALF, HEAD)), shaped((1, 16 * HALF), F32)],
        in_specs=[whole, whole],
        out_specs=[
            pl.BlockSpec((TILE // HALF, HALF, HEAD), lambda i: (i, 0, 0)),
            pl.BlockSpec((1, TILE), lambda i: (0, i)),
        ],
        scratch_shapes=[pltpu.VMEM((HEAD, 32 * HALF), BF)],
        compiler_params=params(),
        cost_estimate=cost(4 * 1024 * 2048 * 256, 3 * 1024 * 1024),
    )(mine, other)


def backward_kernel(
    mine_ref, other_ref, out_ref, grad_ref, lse_ref, gq_ref, own_ref, far_ref, kt_ref, gk_ref, gv_ref
):
    step = pl.program_id(0)
    count = 16 * HALF

    @pl.when(step == 0)
    def _():
        kt_ref[:, :count] = rows_of(mine_ref, 1).T
        kt_ref[:, count:] = rows_of(other_ref, 1).T
        gk_ref[...] = jnp.zeros_like(gk_ref)
        gv_ref[...] = jnp.zeros_like(gv_ref)

    q = mine_ref[pl.ds(step * (TILE // HALF), TILE // HALF), 0].reshape(TILE, HEAD)
    grad = grad_ref[...].reshape(TILE, HEAD)
    out = out_ref[...].reshape(TILE, HEAD)
    delta = jnp.sum((grad.astype(F32) * out.astype(F32)).T, axis=0, keepdims=True)
    lse = lse_ref[...]
    gq = jnp.zeros((HEAD, TILE), F32)
    for part, ref in enumerate((mine_ref, other_ref)):
        span = slice(part * count, (part + 1) * count)
        probs = jnp.exp2(dot_nt(rows_of(ref, 1), q) * SCALE2 - lse)
        slope = (probs * (dot_nt(rows_of(ref, 2), grad) - delta)).astype(BF)
        gv_ref[span] += dot(probs.astype(BF), grad)
        gk_ref[span] += dot(slope, q)
        gq = gq + dot(kt_ref[:, span], slope)
    gq_ref[...] = (gq * SCALE).T.astype(BF).reshape(TILE // HALF, HALF, HEAD)

    @pl.when(step == pl.num_programs(0) - 1)
    def _():
        own_ref[:, 0] = (gk_ref[:count] * SCALE).reshape(16, HALF, HEAD)
        own_ref[:, 1] = gv_ref[:count].reshape(16, HALF, HEAD)
        far_ref[:, 0] = (gk_ref[count:] * SCALE).astype(BF).reshape(16, HALF, HEAD)
        far_ref[:, 1] = gv_ref[count:].astype(BF).reshape(16, HALF, HEAD)


def attention_backward(mine, other, out, grad, lse):
    whole = pl.BlockSpec((16, 3, HALF, HEAD), lambda i: (0, 0, 0, 0))
    part = pl.BlockSpec((TILE // HALF, HALF, HEAD), lambda i: (i, 0, 0))
    both = pl.BlockSpec((16, 2, HALF, HEAD), lambda i: (0, 0, 0, 0))
    return pl.pallas_call(
        backward_kernel,
        grid=(16 * HALF // TILE,),
        out_shape=[
            shaped((16, HALF, HEAD)),
            shaped((16, 2, HALF, HEAD), F32),
            shaped((16, 2, HALF, HEAD)),
        ],
        in_specs=[whole, whole, part, part, pl.BlockSpec((1, TILE), lambda i: (0, i))],
        out_specs=[part, both, both],
        scratch_shapes=[
            pltpu.VMEM((HEAD, 32 * HALF), BF),
            pltpu.VMEM((32 * HALF, HEAD), F32),
            pltpu.VMEM((32 * HALF, HEAD), F32),
        ],
        compiler_params=params(),
        cost_estimate=cost(10 * 1024 * 2048 * 256, 6 * 1024 * 1024),
    )(mine, other, out, grad, lse)


def row_index(shape):
    return lax.broadcasted_iota(jnp.int32, shape, 0)


def shifted_down(block, first):
    return jnp.where(row_index(block.shape) == 0, first, pltpu.roll(block, 1, 0))


def shifted_up(block, last):
    rows = block.shape[0]
    return jnp.where(row_index(block.shape) == rows - 1, last, pltpu.roll(block, rows - 1, 0))


OFFSETS = (0, 3, 1, 2)


def lanes(core, width):
    return pl.ds(pl.multiple_of(core * width, 128), width)


def up_kernel(at_ref, att_ref, res_ref, *refs):
    w_own, w_far = refs[:4], refs[4:8]
    c_own, c_far, mixed_ref, even_ref, odd_ref, fwd_ref, bwd_ref, acc_ref, y_ref = refs[8:]
    core, y = at_ref[0], at_ref[1]
    acc_ref[...] = res_ref[...].astype(F32)
    for k, off in enumerate(OFFSETS):
        head = 2 * lax.rem(y + off, 4)
        for j in range(2):
            block = att_ref[:, head + j].reshape(TOK, HEAD)
            rows = slice(j * HEAD, (j + 1) * HEAD)
            acc_ref[:, lanes(core, WCOLS)] += dot(block, w_own[k][rows])
            acc_ref[:, lanes(1 - core, WCOLS)] += dot(block, w_far[k][rows])
    mixed = acc_ref[...].astype(BF)
    mixed_ref[...] = mixed
    y_ref[:, lanes(core, CCOLS)] = dot(mixed, c_own[...])
    y_ref[:, lanes(1 - core, CCOLS)] = dot(mixed, c_far[...])
    y0, y1, y2, y3, y4 = (y_ref[:, t * CH : (t + 1) * CH] for t in range(TAPS))
    zero = jnp.zeros((1, CH), F32)
    low, high = y0 + y1, y3 + y4
    even_ref[...] = y2 + y3 + shifted_down(low, zero) + shifted_up(y4, zero)
    odd_ref[...] = y1 + y2 + shifted_down(y0, zero) + shifted_up(high, zero)
    fwd_ref[0:1] = low[TOK - 1 :]
    fwd_ref[1:2] = y0[TOK - 1 :]
    bwd_ref[0:1] = y4[:1]
    bwd_ref[1:2] = high[:1]


def project_up(at, att, residual, w_own, w_far, c_own, c_far):
    return pl.pallas_call(
        up_kernel,
        out_shape=[
            shaped((TOK, WIDTH)),
            shaped((TOK, CH), F32),
            shaped((TOK, CH), F32),
            shaped((2, CH), F32),
            shaped((2, CH), F32),
        ],
        in_specs=[SMEM] + [VMEM] * 12,
        out_specs=[VMEM] * 5,
        scratch_shapes=[pltpu.VMEM((TOK, WIDTH), F32), pltpu.VMEM((TOK, 2 * CCOLS), F32)],
        compiler_params=params(),
        cost_estimate=cost(2 * TOK * WIDTH * 3584, WIDTH * 3584 * 2),
    )(at, att, residual, *w_own, *w_far, c_own, c_far)


def gelu_kernel(even_ref, odd_ref, prev_ref, next_ref, skip_ref, cot_ref, dec_ref, gp_ref, first_ref, last_ref):
    for j, ref in enumerate((even_ref, odd_ref)):
        span = slice(j * CH, (j + 1) * CH)
        pre = ref[...]
        row = row_index(pre.shape)
        pre = pre + jnp.where(row == 0, prev_ref[j : j + 1], 0.0)
        pre = pre + jnp.where(row == TOK - 1, next_ref[j : j + 1], 0.0)
        tanh = jnp.tanh(ROOT * (pre + CUBIC * pre * pre * pre))
        act = 0.5 * pre * (1.0 + tanh)
        slope = 0.5 * (1.0 + tanh) + 0.5 * pre * (1.0 - tanh * tanh) * ROOT * (
            1.0 + 3.0 * CUBIC * pre * pre
        )
        dec_ref[:, span] = (act + skip_ref[:, span].astype(F32)).astype(BF)
        grad = (cot_ref[:, span].astype(F32) * slope).astype(BF)
        gp_ref[:, span] = grad
        wide = grad.astype(F32)
        first_ref[:, span] = wide[:1]
        last_ref[:, span] = wide[TOK - 1 :]


def gelu(even, odd, prev, nxt, skip, cot):
    return pl.pallas_call(
        gelu_kernel,
        out_shape=[
            shaped((TOK, 2 * CH)),
            shaped((TOK, 2 * CH)),
            shaped((1, 2 * CH), F32),
            shaped((1, 2 * CH), F32),
        ],
        in_specs=[VMEM] * 6,
        out_specs=[VMEM] * 4,
        compiler_params=params(),
        cost_estimate=cost(TOK * 768 * 30, TOK * 768 * 12),
    )(even, odd, prev, nxt, skip, cot)


def down_kernel(at_ref, gp_ref, prev_ref, next_ref, *refs):
    w_own, w_far = refs[:4], refs[4:8]
    c_own, c_far, gm_ref, gatt_ref, gm_keep, gm_send, g_keep, g_send, g_ref = refs[8:]
    core, y = at_ref[0], at_ref[1]
    e, o = gp_ref[:, :CH].astype(F32), gp_ref[:, CH:].astype(F32)
    e_up, o_up = shifted_up(e, next_ref[:, :CH]), shifted_up(o, next_ref[:, CH:])
    e_dn, o_dn = shifted_down(e, prev_ref[:, :CH]), shifted_down(o, prev_ref[:, CH:])
    for t, block in enumerate((e_up + o_up, o + e_up, e + o, o_dn + e, e_dn + o_dn)):
        g_ref[:, t * CH : (t + 1) * CH] = block.astype(BF)
    g_ref[:, TAPS * CH :] = jnp.zeros((TOK, 2 * CCOLS - TAPS * CH), BF)
    own, far = g_ref[:, lanes(core, CCOLS)], g_ref[:, lanes(1 - core, CCOLS)]
    g_keep[...] = own
    g_send[...] = far
    gm_ref[...] = (dot_nt(own, c_own[...]) + dot_nt(far, c_far[...])).astype(BF)
    own, far = gm_ref[:, lanes(core, WCOLS)], gm_ref[:, lanes(1 - core, WCOLS)]
    gm_keep[...] = own
    gm_send[...] = far
    for k, off in enumerate(OFFSETS):
        head = 2 * lax.rem(y + off, 4)
        for j in range(2):
            rows = slice(j * HEAD, (j + 1) * HEAD)
            block = dot_nt(own, w_own[k][rows]) + dot_nt(far, w_far[k][rows])
            gatt_ref[:, head + j] = block.astype(BF).reshape(2, HALF, HEAD)


def project_down(at, gp, prev, nxt, w_own, w_far, c_own, c_far):
    return pl.pallas_call(
        down_kernel,
        out_shape=[
            shaped((TOK, WIDTH)),
            shaped((2, HEADS, HALF, HEAD)),
            shaped((TOK, WCOLS)),
            shaped((TOK, WCOLS)),
            shaped((TOK, CCOLS)),
            shaped((TOK, CCOLS)),
        ],
        in_specs=[SMEM] + [VMEM] * 13,
        out_specs=[VMEM] * 6,
        scratch_shapes=[pltpu.VMEM((TOK, 2 * CCOLS), BF)],
        compiler_params=params(),
        cost_estimate=cost(2 * TOK * WIDTH * 3584, WIDTH * 3584 * 2),
    )(at, gp, prev, nxt, *w_own, *w_far, c_own, c_far)


def terms_kernel(a_ref, a2_ref, m_ref, m2_ref, gm_ref, gm2_ref, g_ref, g2_ref, o_ref):
    step = pl.program_id(0)
    for j in range(2):
        rows = slice(j * HEAD, (j + 1) * HEAD)
        a = a_ref[:, 2 * step + j].reshape(TOK, HEAD).T
        a2 = a2_ref[:, 2 * step + j].reshape(TOK, HEAD).T
        o_ref[rows, :WCOLS] = (dot(a, gm_ref[...]) + dot(a2, gm2_ref[...])).astype(BF)
    o_ref[:, WCOLS:] = (dot(m_ref[...].T, g_ref[...]) + dot(m2_ref[...].T, g2_ref[...])).astype(BF)


def weight_terms(att, att2, mixed, mixed2, gm, gm2, g, g2):
    heads = pl.BlockSpec((2, HEADS, HALF, HEAD), lambda i: (0, 0, 0, 0))
    cols = pl.BlockSpec((TOK, 2 * HEAD), lambda i: (0, i))
    gms = pl.BlockSpec((TOK, WCOLS), lambda i: (0, 0))
    gs = pl.BlockSpec((TOK, CCOLS), lambda i: (0, 0))
    return pl.pallas_call(
        terms_kernel,
        grid=(4,),
        out_shape=shaped((WIDTH, WCOLS + CCOLS)),
        in_specs=[heads, heads, cols, cols, gms, gms, gs, gs],
        out_specs=pl.BlockSpec((2 * HEAD, WCOLS + CCOLS), lambda i: (i, 0)),
        compiler_params=params(),
        cost_estimate=cost(4 * TOK * WIDTH * 1792, WIDTH * 1792 * 2),
    )(att, att2, mixed, mixed2, gm, gm2, g, g2)


def ring(axis, by, size=4):
    return [(i, (i + by) % size) for i in range(size)]


def swap(block, axis="core"):
    return lax.ppermute(block, axis, [(0, 1), (1, 0)])


def exchange(block, axis):
    return lax.all_to_all(block, axis, split_axis=0, concat_axis=0, tiled=True)


def neighbours(to_next, to_prev):
    up = [(i, i + 1) for i in range(15)]
    return (
        lax.ppermute(to_next, SEQ, up),
        lax.ppermute(to_prev, SEQ, [(b, a) for a, b in up]),
    )


def gathered_pieces(block):
    at = lax.axis_index("zh")
    later = [lax.ppermute(block, "zh", ring("zh", by)) for by in (3, 2, 1)]
    around = jnp.stack([block] + later + [block] + later[:2])
    piece = lax.dynamic_slice_in_dim(around, lax.rem(4 - at, 4), 4, axis=0)
    piece = piece.reshape(4 * block.shape[0], block.shape[1])
    return [piece] + [lax.ppermute(piece, "y", ring("y", (4 - off) % 4)) for off in OFFSETS[1:]]


def body(queries, keys, values, residual, out_weight, conv_weight, skip, cotangent):
    core = lax.axis_index("core")
    at = jnp.stack([core, lax.axis_index("y")]).astype(jnp.int32)

    conv_rows = jnp.pad(
        conv_weight.transpose(1, 0, 2).reshape(-1, TAPS * CH), ((0, 0), (0, 2 * CCOLS - TAPS * CH))
    )
    c_own = lax.all_gather(
        lax.dynamic_slice_in_dim(conv_rows, core * CCOLS, CCOLS, axis=1), SEQ, axis=0, tiled=True
    )
    w_own = gathered_pieces(lax.dynamic_slice_in_dim(out_weight, core * WCOLS, WCOLS, axis=1))
    w_far = [swap(piece) for piece in w_own]
    c_far = swap(c_own)

    packed = exchange(pack(queries[0], keys[0], values[0]), "core")
    mine = exchange(packed.reshape(16, 3, HALF, HEAD), SEQ)
    other = swap(mine)
    out, lse = attention_forward(mine, other)
    att = exchange(exchange(out, SEQ).reshape(2, HEADS, HALF, HEAD), "core")

    mixed, even, odd, to_next, to_prev = project_up(
        at, att, residual[0], w_own, w_far, c_own, c_far
    )
    prev, nxt = neighbours(to_next, to_prev)
    decoded, gp, first, last = gelu(
        even, odd, prev, nxt, skip[0].reshape(TOK, 2 * CH), cotangent[0].reshape(TOK, 2 * CH)
    )
    prev, nxt = neighbours(last, first)
    gm, gatt, gm_keep, gm_send, g_keep, g_send = project_down(
        at, gp, prev, nxt, w_own, w_far, c_own, c_far
    )

    term = weight_terms(
        att, swap(att), mixed, swap(mixed), gm_keep, swap(gm_send), g_keep, swap(g_send)
    )
    columns = WCOLS + CCOLS
    term = term.reshape(16, 4, 24, columns).transpose(1, 0, 2, 3).reshape(4 * 16 * 24, columns)
    part = lax.psum_scatter(term, "x", scatter_dimension=0, tiled=True)
    part = part.reshape(4, 4, 24, columns)
    part = jnp.sum(exchange(part, "y").astype(F32), axis=0).astype(BF)
    part = jnp.sum(exchange(part, "zh").astype(F32), axis=0).astype(BF)
    part = (part.astype(F32) + swap(part, "zl").astype(F32)).astype(BF)
    total = exchange(jnp.broadcast_to(part[None], (4, 24, columns)), "x").reshape(96, columns)

    grad = exchange(exchange(gatt, "core").reshape(16, HALF, HEAD), SEQ)
    gq, own, far = attention_backward(mine, other, out, grad, lse)
    both = (own + swap(far).astype(F32)).astype(BF)
    back = exchange(jnp.concatenate([gq[:, None], both], axis=1), SEQ)
    gq, gk, gv = unpack(exchange(back.reshape(2, HEADS, 3, HALF, HEAD), "core"))

    total_far = swap(total)
    low = jnp.where(core == 0, total, total_far)
    high = jnp.where(core == 0, total_far, total)
    grad_out = jnp.concatenate([low[:, :WCOLS], high[:, :WCOLS]], axis=1).astype(F32)
    grad_conv = jnp.concatenate([low[:, WCOLS:], high[:, WCOLS:]], axis=1)[:, : TAPS * CH]
    grad_conv = grad_conv.reshape(96, TAPS, CH).transpose(1, 0, 2).astype(F32)
    return (
        decoded.reshape(1, 2 * TOK, CH),
        gq[None],
        gk[None],
        gv[None],
        gm[None],
        grad_out,
        grad_conv,
    )


def solution(mesh):
    grid = Mesh(mesh.devices.reshape(2, 4, 2, 4, 4), ("zl", "x", "core", "y", "zh"))
    dp = ("zl", "x", "core")
    tokens = P(dp, SEQ, None)
    in_specs = (tokens, tokens, tokens, tokens, P(SEQ, None), P(None, SEQ, None), tokens, tokens)
    out_specs = (tokens, tokens, tokens, tokens, tokens, P(SEQ, None), P(None, SEQ, None))
    return jax.shard_map(body, mesh=grid, in_specs=in_specs, out_specs=out_specs, check_vma=False)
```

time: 638 us -> 437 us (0.68); the launches traced: 627 us -> 436 us
  waiting for transfers between devices: 359 us -> 216 us
  matrix products: 54.5 us -> 0 us
  Pallas kernels: 0 us -> 51.9 us
  local copies, waits for them, and re-layouts: 53 us -> 26.5 us
  blocking collectives: 63.2 us -> 46.1 us
  other arithmetic: 18.7 us -> 6.07 us
  starting transfers between devices: 64.4 us -> 75 us
    psum x1 -> x0, waiting for transfers between devices: 119 us -> none  [body(): lax.psum(proj_shard.astype(jnp.bfloat16), 'dp').astype(jnp.float32)]
    dot_general x16 -> x0, matrix products: 54.5 us -> none  [the longest x5 10.6 us: body(): lax.dot_general(upsampled[tap_offset + tap_index:tap_offset + tap_index +...]
    pallas_call x0 -> x8, Pallas kernels: none -> 51.9 us  [the longest x1 11.5 us: attention_backward(): pl.pallas_call(backward_kernel, grid=(16 * HALF // TILE,), out_shape=[sha...]
    reduce_scatter x2 -> x1, waiting for transfers between devices: 108 us -> 56.3 us  [body(): part = lax.psum_scatter(term, 'x', scatter_dimension=0, tiled=True)]
    ppermute x4 -> x23, waiting for transfers between devices: 0.37 us -> 34.1 us  [the longest x3 12.7 us: gathered_pieces(): later = [lax.ppermute(block, 'zh', ring('zh', by)) for by in (3, 2, 1)]]
    all_to_all x6 -> x7, waiting for transfers between devices: 76.4 us -> 55.6 us  [exchange(): return lax.all_to_all(block, axis, split_axis=0, concat_axis=0, tiled=True)]
    all_to_all x2 -> x4, blocking collectives: 63.2 us -> 46.1 us  [exchange(): return lax.all_to_all(block, axis, split_axis=0, concat_axis=0, tiled=True)]
    all_gather x2 -> x1, waiting for transfers between devices: 54.5 us -> 69.8 us  [body(): lax.all_gather(lax.dynamic_slice_in_dim(conv_rows, core * CCOLS, CCOLS, a...]
  transfers between devices with their start and end apart: 15 -> 32, of which waited for: 9 -> 14; matrix products, arithmetic and copies ran while one was open for 16% -> 4% of each run, Pallas kernels for 0% -> 8%
where the time goes in v1:
time: 437 us; the launch traced here: 436 us
  waiting for transfers between devices  216 us (49%)
  starting transfers between devices  75 us (17%)
  Pallas kernels  51.9 us (12%)
  blocking collectives  46.1 us (11%)
  local copies, waits for them, and re-layouts  26.5 us (6%)
  between operations  14.3 us (3%)
  other arithmetic  6.07 us (1%)
    all_gather x1, waiting for transfers between devices, body(): lax.all_gather(lax.dynamic_slice_in_dim(conv_rows, core * CCOLS, CCOLS, a...  69.8 us
    reduce_scatter x1, waiting for transfers between devices, body(): part = lax.psum_scatter(term, 'x', scatter_dimension=0, tiled=True)  56.3 us
    all_to_all x7, waiting for transfers between devices, exchange(): return lax.all_to_all(block, axis, split_axis=0, concat_axis=0, tiled=True)  55.6 us
    all_to_all x4, blocking collectives, exchange(): return lax.all_to_all(block, axis, split_axis=0, concat_axis=0, tiled=True)  46.1 us
    all_to_all x7, starting transfers between devices, exchange(): return lax.all_to_all(block, axis, split_axis=0, concat_axis=0, tiled=True)  41.5 us
    ppermute x13, starting transfers between devices, swap(): return lax.ppermute(block, axis, [(0, 1), (1, 0)])  17.2 us
    unnamed x43, local copies, waits for them, and re-layouts  13 us
    ppermute x3, waiting for transfers between devices, gathered_pieces(): later = [lax.ppermute(block, 'zh', ring('zh', by)) for by in (3, 2, 1)]  12.7 us
  transfers between devices with their start and end apart: 32, of which 14 were waited for; matrix products, arithmetic and copies ran while one was open for 4% of the time, Pallas kernels for 8%

profile of v1, /device:TPU:1, one launch (start us, length us, event | category | flops | bytes accessed | tf_op | source)
XLA Modules:
  0.0 435.7 jit_solution(9577099797061395712)
XLA Ops:
  7.2 1.3 copy.21
  9.5 2.7 shard_map.135
  12.2 10.7 %all_to_all.55 = bf16[2,8,3,64,192]{4,3,2,1,0:T(8,128)(2,1)} all-to-all(bf16[2,8,3,64,192]{4,3,2,1,0:T(8,128)(2,1)} %shard_map.135), channel_id=1, replica_groups=mesh['zl'=2,'x'=4,'core'=2,'y'=4,'zh'=4] {'core'}, dimensions={0} | all-to-all | bytes 2359296 | tf_op jit(solution)/shard_map/all_to_all | solution.py:371
  22.8 9.4 %all-to-all-start.1 = ((bf16[16,3,64,192]{3,2,1,0:T(8,128)(2,1)}), bf16[16,3,64,192]{3,2,1,0:T(8,128)(2,1)}, u32[]{:S(2)}, u32[]{:S(2)}) async-start(bf16[16,3,64,192]{3,2,1,0:T(8,128)(2,1)} %bitcast.5), calls=%async_computation.1 | async-start | bytes 3145728 | tf_op jit(solution)/shard_map/all_to_all | solution.py:371
  32.2 69.8 %all-gather.2.cloned.1.call-done.refs_8_ = bf16[1536,1024]{1,0:T(8,128)(2,1)} async-done(((bf16[96,1024]{1,0:T(8,128)(2,1)}), bf16[1536,1024]{1,0:T(8,128)(2,1)}) %all-gather.2.cloned.1.call-update) | async-done | bytes 3145744 | tf_op jit(solution)/shard_map/all_gather | solution.py:398
  102.4 0.7 bitcast_dynamic-update-slice_fusion.5
  103.2 1.4 collective-permute-start.1
  104.6 2.5 collective-permute-start.2
  107.1 9.1 %collective-permute-done.1 = bf16[96,768]{1,0:T(8,128)(2,1)S(1)} collective-permute-done((bf16[96,768]{1,0:T(8,128)(2,1)}, bf16[96,768]{1,0:T(8,128)(2,1)S(1)}, u32[]{:S(2)}, u32[]{:S(2)}) %collective-permute-start.1) | collective-permute-done | bytes 147488 | tf_op jit(solution)/shard_map/ppermute | solution.py:384
  116.9 1.2 collective-permute-done.2
  119.4 2.4 collective-permute-done.3
  121.8 1.6 bitcast_dynamic-update-slice_fusion
  123.4 1.6 bitcast_dynamic-update-slice_fusion.6
  126.3 1.9 constant_dynamic-slice_fusion
  128.2 2.7 collective-permute-start.5
  130.9 1.1 copy-done.17
  132.0 9.3 %shard_map.136 = (bf16[16,64,192]{2,1,0:T(8,128)(2,1)}, f32[1,1024]{1,0:T(1,128)}) custom-call(bf16[16,3,64,192]{3,2,1,0:T(8,128)(2,1)} %all-to-all-done.1.mine_ref, bf16[16,3,64,192]{3,2,1,0:T(8,128)(2,1)} %copy-done.17), custom_call_target="tpu_custom_call" | custom-call | flops 2147483648 | bytes 3145728 | tf_op jit(solution)/shard_map/pallas_call | solution.py:116
  141.4 5.6 %all-to-all-start.2 = ((bf16[16,64,192]{2,1,0:T(8,128)(2,1)}), bf16[16,64,192]{2,1,0:T(8,128)(2,1)}, u32[]{:S(2)}, u32[]{:S(2)}) async-start(bf16[16,64,192]{2,1,0:T(8,128)(2,1)} %get-tuple-element.30.out_ref), calls=%async_computation.2 | async-start | bytes 1048576 | tf_op jit(solution)/shard_map/all_to_all | solution.py:371
  147.0 2.1 collective-permute-start.7
  149.1 11.1 %collective-permute-done.4.refs_1_ = bf16[384,768]{1,0:T(8,128)(2,1)} collective-permute-done((bf16[384,768]{1,0:T(8,128)(2,1)}, bf16[384,768]{1,0:T(8,128)(2,1)}, u32[]{:S(2)}, u32[]{:S(2)}) %collective-permute-start.4) | collective-permute-done | bytes 589856 | tf_op jit(solution)/shard_map/ppermute | solution.py:388
  160.2 2.8 collective-permute-start.8
  164.1 4.9 %all-to-all-start.3 = ((bf16[2,8,64,192]{3,2,1,0:T(8,128)(2,1)}), bf16[2,8,64,192]{3,2,1,0:T(8,128)(2,1)}, u32[]{:S(2)}, u32[]{:S(2)}) async-start(bf16[2,8,64,192]{3,2,1,0:T(8,128)(2,1)} %bitcast.6), calls=%async_computation.3 | async-start | bytes 1048576 | tf_op jit(solution)/shard_map/all_to_all | solution.py:371
  169.0 1.5 all-to-all-done.3.att_ref.a_ref
  170.5 1.7 copy-done
  172.2 7.5 %shard_map.137 = (bf16[128,1536]{1,0:T(8,128)(2,1)}, f32[128,384]{1,0:T(8,128)}, f32[128,384]{1,0:T(8,128)}, f32[2,384]{1,0:T(2,128)}, f32[2,384]{1,0:T(2,128)}) custom-call(s32[2]{0:T(128)} %pad_add_fusion.at_ref, bf16[2,8,64,192]{3,2,1,0:T(8,128)(2,1)} %all-to-all-done.3.att_ref.a_ref, bf16[128,1536]{1,0:T(8,128)(2,1)} %bitcast.48, ...), custom_call_target="tpu_custom_call" | custom-call | flops 1409286144 | bytes 11010048 | tf_op jit(solution)/shard_map/pallas_call | solution.py:239
  179.7 3.7 collective-permute-start.12
  183.4 1.3 collective-permute-start.13
  184.7 0.7 reshape_squeeze.6.skip_ref
  185.5 0.7 reshape_squeeze.7.cot_ref
  186.2 2.6 collective-permute-done.13.next_ref
  189.5 2.3 shard_map.138
  191.8 3.4 collective-permute-start.14
  195.2 1.3 collective-permute-start.15
  196.5 2.1 collective-permute-start.17
  198.7 1.9 collective-permute-done.15.next_ref
  201.2 9.1 %shard_map.139 = (bf16[128,1536]{1,0:T(8,128)(2,1)}, bf16[2,8,64,192]{3,2,1,0:T(8,128)(2,1)}, bf16[128,768]{1,0:T(8,128)(2,1)}, bf16[128,768]{1,0:T(8,128)(2,1)}...) custom-call(s32[2]{0:T(128)} %pad_add_fusion.at_ref, bf16[128,768]{1,0:T(8,128)(2,1)} %get-tuple-element.36.gp_ref, ...), custom_call_target="tpu_custom_call" | custom-call | flops 1409286144 | bytes 11010048 | tf_op jit(solution)/shard_map/pallas_call | solution.py:318
  210.3 3.3 collective-permute-start.20
  213.7 1.5 collective-permute-done.19.gm2_ref
  216.2 6.8 %shard_map.142 = bf16[1536,1792]{1,0:T(8,128)(2,1)} custom-call(bf16[2,8,64,192]{3,2,1,0:T(8,128)(2,1)} %all-to-all-done.3.att_ref.a_ref, bf16[2,8,64,192]{3,2,1,0:T(8,128)(2,1)} %copy-done.1, bf16[128,1536]{1,0:T(8,128)(2,1)} %get-tuple-element.48.m_ref, bf16[128,1536]{1,0:T(8,128)(2,1)} %copy-done.6, bf16[128,768]{1,0:T(8,128)(2,1)} %get-tuple-element.49.gm_ref, ...), custom_call_target="tpu_custom_call" | custom-call | flops 1409286144 | bytes 5505024 | tf_op jit(solution)/shard_map/pallas_call | solution.py:351
  223.0 5.4 %copy.23 = bf16[16,4,24,1792]{3,2,0,1:T(8,128)(2,1)} copy(bf16[16,4,24,1792]{3,2,1,0:T(8,128)(2,1)} %bitcast.41) | data formatting | bytes 11010048 | tf_op jit(solution)/shard_map/reshape | solution.py:427
  228.4 1.0 copy-done.2
  229.4 4.9 %all_to_all.56 = bf16[2,8,64,192]{3,2,1,0:T(8,128)(2,1)} all-to-all(bf16[2,8,64,192]{3,2,1,0:T(8,128)(2,1)S(1)} %copy-done.2), channel_id=1, replica_groups=mesh['zl'=2,'x'=4,'core'=2,'y'=4,'zh'=4] {'core'}, dimensions={0} | all-to-all | bytes 786432 | tf_op jit(solution)/shard_map/all_to_all | solution.py:371
  234.3 56.3 %reduce-scatter.2.cloned.1.call-done = bf16[384,1792]{1,0:T(8,128)(2,1)} async-done(((bf16[1536,1792]{1,0:T(8,128)(2,1)}), bf16[384,1792]{1,0:T(8,128)(2,1)}) %reduce-scatter.2.cloned.1.call-update) | async-done | bytes 1376272 | tf_op jit(solution)/shard_map/reduce_scatter | solution.py:428
  290.6 21.5 %all_to_all.57 = bf16[4,4,24,1792]{3,2,1,0:T(8,128)(2,1)S(1)} all-to-all(bf16[4,4,24,1792]{3,2,1,0:T(8,128)(2,1)} %bitcast.45), channel_id=1, replica_groups=mesh['zl'=2,'x'=4,'core'=2,'y'=4,'zh'=4] {'y'}, dimensions={0} | all-to-all | bytes 2752512 | tf_op jit(solution)/shard_map/all_to_all | solution.py:371
  312.0 7.4 %all-to-all-start.5 = ((bf16[16,64,192]{2,1,0:T(8,128)(2,1)}), bf16[16,64,192]{2,1,0:T(8,128)(2,1)S(1)}, u32[]{:S(2)}, u32[]{:S(2)}) async-start(bf16[16,64,192]{2,1,0:T(8,128)(2,1)} %bitcast.15), calls=%async_computation.5 | async-start | bytes 1048576 | tf_op jit(solution)/shard_map/all_to_all | solution.py:371
  319.5 1.0 reduce_sum.24
  320.5 16.3 %all-to-all-done.5.grad_ref = bf16[16,64,192]{2,1,0:T(8,128)(2,1)S(1)} async-done(((bf16[16,64,192]{2,1,0:T(8,128)(2,1)}), bf16[16,64,192]{2,1,0:T(8,128)(2,1)S(1)}, u32[]{:S(2)}, u32[]{:S(2)}) %all-to-all-start.5) | async-done | bytes 393248 | tf_op jit(solution)/shard_map/all_to_all | solution.py:371
  336.8 3.5 all-to-all-start.9
  340.3 11.5 %shard_map.140 = (bf16[16,64,192]{2,1,0:T(8,128)(2,1)}, f32[16,2,64,192]{3,2,1,0:T(8,128)}, bf16[16,2,64,192]{3,2,1,0:T(8,128)(2,1)}) custom-call(bf16[16,3,64,192]{3,2,1,0:T(8,128)(2,1)} %all-to-all-done.1.mine_ref, bf16[16,3,64,192]{3,2,1,0:T(8,128)(2,1)} %copy-done.17, bf16[16,64,192]{2,1,0:T(8,128)(2,1)} %get-tuple-element.30.out_ref, ...), custom_call_target="tpu_custom_call" | custom-call | flops 5368709120 | bytes 6291456 | tf_op jit(solution)/shard_map/pallas_call | solution.py:171
  351.8 2.5 collective-permute-start.16
  354.5 4.1 collective-permute-done.21
  358.6 0.8 broadcast_in_dim.26
  359.4 3.5 all-to-all-start.10
  362.9 2.0 add_convert_fusion
  364.9 1.4 pad_maximum_fusion
  366.3 3.0 all-to-all-done.10
  369.3 7.3 %all-to-all-start.6 = ((bf16[16,3,64,192]{3,2,1,0:T(8,128)(2,1)}), bf16[16,3,64,192]{3,2,1,0:T(8,128)(2,1)S(1)}, u32[]{:S(2)}, u32[]{:S(2)}) async-start(bf16[16,3,64,192]{3,2,1,0:T(8,128)(2,1)} %pad_maximum_fusion), calls=%async_computation.6 | async-start | bytes 3145728 | tf_op jit(solution)/shard_map/all_to_all | solution.py:371
  376.6 2.4 collective-permute-start.22
  379.0 0.7 reshape.55
  379.7 34.9 %all-to-all-done.6 = bf16[16,3,64,192]{3,2,1,0:T(8,128)(2,1)S(1)} async-done(((bf16[16,3,64,192]{3,2,1,0:T(8,128)(2,1)}), bf16[16,3,64,192]{3,2,1,0:T(8,128)(2,1)S(1)}, u32[]{:S(2)}, u32[]{:S(2)}) %all-to-all-start.6) | async-done | bytes 1179680 | tf_op jit(solution)/shard_map/all_to_all | solution.py:371
  414.6 9.1 %all_to_all.58.x_ref = bf16[2,8,3,64,192]{4,3,2,1,0:T(8,128)(2,1)} all-to-all(bf16[2,8,3,64,192]{4,3,2,1,0:T(8,128)(2,1)S(1)} %bitcast.42), channel_id=1, replica_groups=mesh['zl'=2,'x'=4,'core'=2,'y'=4,'zh'=4] {'core'}, dimensions={0} | all-to-all | bytes 2359296 | tf_op jit(solution)/shard_map/all_to_all | solution.py:371
  423.7 2.5 shard_map.141
  426.8 1.2 copy.25
  428.0 0.9 maximum_convert_fusion
  (81 shorter events, 8.9 us)
Async XLA Ops:
  7.2 94.8 %all-gather.2.cloned.1.call-start = ((), (), s32[]{:S(2)}) async-start(), calls=%async_computation.12 | async-start | bytes 3342336 | tf_op jit(solution)/shard_map/all_gather | solution.py:398
  22.8 79.6 %copy-start.12 = (bf16[96,1536]{1,0:T(8,128)(2,1)S(1)}, bf16[96,1536]{1,0:T(8,128)(2,1)}, u32[]{:S(2)}) copy-start(bf16[96,1536]{1,0:T(8,128)(2,1)} %param.12) | copy-start | bytes 884740
  22.8 95.9 %all-to-all-start.1 = ((bf16[16,3,64,192]{3,2,1,0:T(8,128)(2,1)}), bf16[16,3,64,192]{3,2,1,0:T(8,128)(2,1)}, u32[]{:S(2)}, u32[]{:S(2)}) async-start(bf16[16,3,64,192]{3,2,1,0:T(8,128)(2,1)} %bitcast.5), calls=%async_computation.1 | async-start | bytes 3145728 | tf_op jit(solution)/shard_map/all_to_all | solution.py:371
  102.0 68.5 %collective-permute-start.11 = (bf16[1536,1024]{1,0:T(8,128)(2,1)}, bf16[1536,1024]{1,0:T(8,128)(2,1)S(1)}, u32[]{:S(2)}, u32[]{:S(2)}) collective-permute-start(bf16[1536,1024]{1,0:T(8,128)(2,1)} %all-gather.2.cloned.1.call-done.refs_8_), channel_id=1, source_target_pairs={{0,16},{16,0},{1,17},{17,1},{2,18},{18,2},{3,19},{19,3},{4,20},{20... | collective-permute-start | bytes 9437192 | tf_op jit(solution)/shard_map/ppermute | solution.py:367
  103.2 13.0 %collective-permute-start.1 = (bf16[96,768]{1,0:T(8,128)(2,1)}, bf16[96,768]{1,0:T(8,128)(2,1)S(1)}, u32[]{:S(2)}, u32[]{:S(2)}) collective-permute-start(bf16[96,768]{1,0:T(8,128)(2,1)} %get-tuple-element.68), channel_id=1, source_target_pairs={{0,3},{1,0},{2,1},{3,2},{4,7},{5,4},{6,5},{7,6},{8,11},{9,8},{10,9... | collective-permute-start | bytes 442376 | tf_op jit(solution)/shard_map/ppermute | solution.py:384
  104.6 13.5 %collective-permute-start.2 = (bf16[96,768]{1,0:T(8,128)(2,1)}, bf16[96,768]{1,0:T(8,128)(2,1)S(1)}, u32[]{:S(2)}, u32[]{:S(2)}) collective-permute-start(bf16[96,768]{1,0:T(8,128)(2,1)} %get-tuple-element.68), channel_id=1, source_target_pairs={{0,2},{1,3},{2,0},{3,1},{4,6},{5,7},{6,4},{7,5},{8,10},{9,11},{10,... | collective-permute-start | bytes 442376 | tf_op jit(solution)/shard_map/ppermute | solution.py:384
  107.1 14.7 %collective-permute-start.3 = (bf16[96,768]{1,0:T(8,128)(2,1)}, bf16[96,768]{1,0:T(8,128)(2,1)}, u32[]{:S(2)}, u32[]{:S(2)}) collective-permute-start(bf16[96,768]{1,0:T(8,128)(2,1)} %get-tuple-element.68), channel_id=1, source_target_pairs={{0,1},{1,2},{2,3},{3,0},{4,5},{5,6},{6,7},{7,4},{8,9},{9,10},{10,1... | collective-permute-start | bytes 442376 | tf_op jit(solution)/shard_map/ppermute | solution.py:384
  118.8 12.1 %collective-permute-start = (bf16[16,3,64,192]{3,2,1,0:T(8,128)(2,1)}, bf16[16,3,64,192]{3,2,1,0:T(8,128)(2,1)S(1)}, u32[]{:S(2)}, u32[]{:S(2)}) collective-permute-start(bf16[16,3,64,192]{3,2,1,0:T(8,128)(2,1)} %all-to-all-done.1.mine_ref), channel_id=1, source_target_pairs={{0,16},{16,0},{1,17},{17,1},{2,18},{18,2},{3,19},{19,3},{4,20},{20... | collective-permute-start | bytes 3538952 | tf_op jit(solution)/shard_map/ppermute | solution.py:367
  128.2 32.0 %collective-permute-start.4 = (bf16[384,768]{1,0:T(8,128)(2,1)}, bf16[384,768]{1,0:T(8,128)(2,1)}, u32[]{:S(2)}, u32[]{:S(2)}) collective-permute-start(bf16[384,768]{1,0:T(8,128)(2,1)} %bitcast.12.refs_0_), channel_id=1, source_target_pairs={{0,4},{4,8},{8,12},{12,0},{1,5},{5,9},{9,13},{13,1},{2,6},{6,10},{... | collective-permute-start | bytes 1769480 | tf_op jit(solution)/shard_map/ppermute | solution.py:388
  128.2 34.8 %collective-permute-start.5 = (bf16[384,768]{1,0:T(8,128)(2,1)}, bf16[384,768]{1,0:T(8,128)(2,1)}, u32[]{:S(2)}, u32[]{:S(2)}) collective-permute-start(bf16[384,768]{1,0:T(8,128)(2,1)} %bitcast.12.refs_0_), channel_id=1, source_target_pairs={{0,12},{4,0},{8,4},{12,8},{1,13},{5,1},{9,5},{13,9},{2,14},{6,2},{... | collective-permute-start | bytes 1769480 | tf_op jit(solution)/shard_map/ppermute | solution.py:388
  130.9 32.1 %collective-permute-start.6 = (bf16[384,768]{1,0:T(8,128)(2,1)}, bf16[384,768]{1,0:T(8,128)(2,1)}, u32[]{:S(2)}, u32[]{:S(2)}) collective-permute-start(bf16[384,768]{1,0:T(8,128)(2,1)} %bitcast.12.refs_0_), channel_id=1, source_target_pairs={{0,8},{4,12},{8,0},{12,4},{1,9},{5,13},{9,1},{13,5},{2,10},{6,14},... | collective-permute-start | bytes 1769480 | tf_op jit(solution)/shard_map/ppermute | solution.py:388
  130.9 1.1 copy-start.17
  141.4 22.7 %all-to-all-start.2 = ((bf16[16,64,192]{2,1,0:T(8,128)(2,1)}), bf16[16,64,192]{2,1,0:T(8,128)(2,1)}, u32[]{:S(2)}, u32[]{:S(2)}) async-start(bf16[16,64,192]{2,1,0:T(8,128)(2,1)} %get-tuple-element.30.out_ref), calls=%async_computation.2 | async-start | bytes 1048576 | tf_op jit(solution)/shard_map/all_to_all | solution.py:371
  147.0 22.0 %collective-permute-start.7 = (bf16[384,768]{1,0:T(8,128)(2,1)}, bf16[384,768]{1,0:T(8,128)(2,1)}, u32[]{:S(2)}, u32[]{:S(2)}) collective-permute-start(bf16[384,768]{1,0:T(8,128)(2,1)} %bitcast.12.refs_0_), channel_id=1, source_target_pairs={{0,16},{16,0},{1,17},{17,1},{2,18},{18,2},{3,19},{19,3},{4,20},{20... | collective-permute-start | bytes 1769480 | tf_op jit(solution)/shard_map/ppermute | solution.py:367
  160.2 8.8 %collective-permute-start.8 = (bf16[384,768]{1,0:T(8,128)(2,1)}, bf16[384,768]{1,0:T(8,128)(2,1)}, u32[]{:S(2)}, u32[]{:S(2)}) collective-permute-start(bf16[384,768]{1,0:T(8,128)(2,1)} %collective-permute-done.4.refs_1_), channel_id=1, source_target_pairs={{0,16},{16,0},{1,17},{17,1},{2,18},{18,2},{3,19},{19,3},{4,20},{20... | collective-permute-start | bytes 1769480 | tf_op jit(solution)/shard_map/ppermute | solution.py:367
  163.0 6.0 %collective-permute-start.9 = (bf16[384,768]{1,0:T(8,128)(2,1)}, bf16[384,768]{1,0:T(8,128)(2,1)}, u32[]{:S(2)}, u32[]{:S(2)}) collective-permute-start(bf16[384,768]{1,0:T(8,128)(2,1)} %collective-permute-done.5.refs_2_), channel_id=1, source_target_pairs={{0,16},{16,0},{1,17},{17,1},{2,18},{18,2},{3,19},{19,3},{4,20},{20... | collective-permute-start | bytes 1769480 | tf_op jit(solution)/shard_map/ppermute | solution.py:367
  163.1 6.0 %collective-permute-start.10 = (bf16[384,768]{1,0:T(8,128)(2,1)}, bf16[384,768]{1,0:T(8,128)(2,1)}, u32[]{:S(2)}, u32[]{:S(2)}) collective-permute-start(bf16[384,768]{1,0:T(8,128)(2,1)} %collective-permute-done.6.refs_3_), channel_id=1, source_target_pairs={{0,16},{16,0},{1,17},{17,1},{2,18},{18,2},{3,19},{19,3},{4,20},{20... | collective-permute-start | bytes 1769480 | tf_op jit(solution)/shard_map/ppermute | solution.py:367
  164.1 6.4 %all-to-all-start.3 = ((bf16[2,8,64,192]{3,2,1,0:T(8,128)(2,1)}), bf16[2,8,64,192]{3,2,1,0:T(8,128)(2,1)}, u32[]{:S(2)}, u32[]{:S(2)}) async-start(bf16[2,8,64,192]{3,2,1,0:T(8,128)(2,1)} %bitcast.6), calls=%async_computation.3 | async-start | bytes 1048576 | tf_op jit(solution)/shard_map/all_to_all | solution.py:371
  169.0 121.5 %reduce-scatter.2.cloned.1.call-start = ((), (), s32[]{:S(2)}) async-start(), calls=%async_computation.13 | async-start | bytes 6881280 | tf_op jit(solution)/shard_map/reduce_scatter | solution.py:428
  170.5 1.7 copy-start
  172.2 12.5 %copy-start.8 = (bf16[1,256,384]{2,1,0:T(8,128)(2,1)S(1)}, bf16[1,256,384]{2,1,0:T(8,128)(2,1)}, u32[]{:S(2)}) copy-start(bf16[1,256,384]{2,1,0:T(8,128)(2,1)} %param.14) | copy-start | bytes 589828
  172.2 13.3 %copy-start.9 = (bf16[1,256,384]{2,1,0:T(8,128)(2,1)S(1)}, bf16[1,256,384]{2,1,0:T(8,128)(2,1)}, u32[]{:S(2)}) copy-start(bf16[1,256,384]{2,1,0:T(8,128)(2,1)} %param.15) | copy-start | bytes 589828
  179.7 18.9 %copy-start.5 = (bf16[128,1536]{1,0:T(8,128)(2,1)S(1)}, bf16[128,1536]{1,0:T(8,128)(2,1)}, u32[]{:S(2)}) copy-start(bf16[128,1536]{1,0:T(8,128)(2,1)} %get-tuple-element.48.m_ref) | copy-start | bytes 1179652
  179.7 6.5 %collective-permute-start.12 = (f32[2,384]{1,0:T(2,128)}, f32[2,384]{1,0:T(2,128)S(1)}, u32[]{:S(2)}, u32[]{:S(2)}) collective-permute-start(f32[2,384]{1,0:T(2,128)} %get-tuple-element.33), channel_id=1, source_target_pairs={{0,1},{1,2},{2,3},{3,4},{4,5},{5,6},{6,7},{7,8},{8,9},{9,10},{10,1... | collective-permute-start | bytes 9224 | tf_op jit(solution)/shard_map/ppermute | solution.py:377
  183.4 5.4 %collective-permute-start.13 = (f32[2,384]{1,0:T(2,128)}, f32[2,384]{1,0:T(2,128)S(1)}, u32[]{:S(2)}, u32[]{:S(2)}) collective-permute-start(f32[2,384]{1,0:T(2,128)} %get-tuple-element.34), channel_id=1, source_target_pairs={{1,0},{2,1},{3,2},{4,3},{5,4},{6,5},{7,6},{8,7},{9,8},{10,9},{11,1... | collective-permute-start | bytes 9224 | tf_op jit(solution)/shard_map/ppermute | solution.py:378
  186.2 2.6 copy-start.15
  188.9 0.6 copy-start.16
  191.8 7.0 %collective-permute-start.14 = (f32[1,768]{1,0:T(1,128)}, f32[1,768]{1,0:T(1,128)S(1)}, u32[]{:S(2)}, u32[]{:S(2)}) collective-permute-start(f32[1,768]{1,0:T(1,128)} %get-tuple-element.37), channel_id=1, source_target_pairs={{0,1},{1,2},{2,3},{3,4},{4,5},{5,6},{6,7},{7,8},{8,9},{9,10},{10,1... | collective-permute-start | bytes 9224 | tf_op jit(solution)/shard_map/ppermute | solution.py:377
  195.2 5.4 %collective-permute-start.15 = (f32[1,768]{1,0:T(1,128)}, f32[1,768]{1,0:T(1,128)S(1)}, u32[]{:S(2)}, u32[]{:S(2)}) collective-permute-start(f32[1,768]{1,0:T(1,128)} %get-tuple-element.38), channel_id=1, source_target_pairs={{1,0},{2,1},{3,2},{4,3},{5,4},{6,5},{7,6},{8,7},{9,8},{10,9},{11,1... | collective-permute-start | bytes 9224 | tf_op jit(solution)/shard_map/ppermute | solution.py:378
  196.5 17.2 %collective-permute-start.17 = (bf16[2,8,64,192]{3,2,1,0:T(8,128)(2,1)}, bf16[2,8,64,192]{3,2,1,0:T(8,128)(2,1)S(1)}, u32[]{:S(2)}, u32[]{:S(2)}) collective-permute-start(bf16[2,8,64,192]{3,2,1,0:T(8,128)(2,1)} %all-to-all-done.3.att_ref.a_ref), channel_id=1, source_target_pairs={{0,16},{16,0},{1,17},{17,1},{2,18},{18,2},{3,19},{19,3},{4,20},{20... | collective-permute-start | bytes 1179656 | tf_op jit(solution)/shard_map/ppermute | solution.py:367
  198.6 16.6 %collective-permute-start.18 = (bf16[128,1536]{1,0:T(8,128)(2,1)S(1)}, bf16[128,1536]{1,0:T(8,128)(2,1)S(1)}, u32[]{:S(2)}, u32[]{:S(2)}) collective-permute-start(bf16[128,1536]{1,0:T(8,128)(2,1)S(1)} %copy-done.5), channel_id=1, source_target_pairs={{0,16},{16,0},{1,17},{17,1},{2,18},{18,2},{3,19},{19,3},{4,20},{20... | collective-permute-start | bytes 1179656 | tf_op jit(solution)/shard_map/ppermute | solution.py:367
  198.7 1.9 copy-start.13
  200.6 0.6 copy-start.14
  210.3 4.9 %collective-permute-start.20 = (bf16[128,1024]{1,0:T(8,128)(2,1)}, bf16[128,1024]{1,0:T(8,128)(2,1)S(1)}, u32[]{:S(2)}, u32[]{:S(2)}) collective-permute-start(bf16[128,1024]{1,0:T(8,128)(2,1)} %get-tuple-element.52), channel_id=1, source_target_pairs={{0,16},{16,0},{1,17},{17,1},{2,18},{18,2},{3,19},{19,3},{4,20},{20... | collective-permute-start | bytes 786440 | tf_op jit(solution)/shard_map/ppermute | solution.py:367
  213.6 1.7 collective-permute-start.19
  213.7 1.6 copy-start.1
  215.3 0.7 copy-start.11
  215.3 0.8 copy-start.7
  215.3 0.9 copy-start.6
  228.3 1.0 copy-start.2
  312.0 24.7 %all-to-all-start.5 = ((bf16[16,64,192]{2,1,0:T(8,128)(2,1)}), bf16[16,64,192]{2,1,0:T(8,128)(2,1)S(1)}, u32[]{:S(2)}, u32[]{:S(2)}) async-start(bf16[16,64,192]{2,1,0:T(8,128)(2,1)} %bitcast.15), calls=%async_computation.5 | async-start | bytes 1048576 | tf_op jit(solution)/shard_map/all_to_all | solution.py:371
  336.8 3.5 copy-start.3
  336.8 17.6 %all-to-all-start.9 = ((bf16[4,24,1792]{2,1,0:T(8,128)(2,1)}), bf16[4,24,1792]{2,1,0:T(8,128)(2,1)S(1)}, u32[]{:S(2)}, u32[]{:S(2)}) async-start(bf16[4,24,1792]{2,1,0:T(8,128)(2,1)} %reduce_sum.24), calls=%async_computation.10 | async-start | bytes 688128 | tf_op jit(solution)/shard_map/all_to_all | solution.py:371
  351.8 11.1 %collective-permute-start.16 = (bf16[16,2,64,192]{3,2,1,0:T(8,128)(2,1)}, bf16[16,2,64,192]{3,2,1,0:T(8,128)(2,1)S(1)}, u32[]{:S(2)}, u32[]{:S(2)}) collective-permute-start(bf16[16,2,64,192]{3,2,1,0:T(8,128)(2,1)} %get-tuple-element.43), channel_id=1, source_target_pairs={{0,16},{16,0},{1,17},{17,1},{2,18},{18,2},{3,19},{19,3},{4,20},{20... | collective-permute-start | bytes 2359304 | tf_op jit(solution)/shard_map/ppermute | solution.py:367
  354.4 4.2 collective-permute-start.21
  359.4 9.9 %all-to-all-start.10 = ((bf16[4,24,1792]{2,1,0:T(8,128)(2,1)}), bf16[4,24,1792]{2,1,0:T(8,128)(2,1)S(1)}, u32[]{:S(2)}, u32[]{:S(2)}) async-start(bf16[4,24,1792]{2,1,0:T(8,128)(2,1)} %broadcast_in_dim.26), calls=%async_computation.11 | async-start | bytes 688128 | tf_op jit(solution)/shard_map/all_to_all | solution.py:371
  362.9 2.0 copy-start.4
  366.3 12.7 %copy-start.10 = (bf16[128,768]{1,0:T(8,128)(2,1)S(1)}, bf16[128,768]{1,0:T(8,128)(2,1)}, u32[]{:S(2)}) copy-start(bf16[128,768]{1,0:T(8,128)(2,1)} %get-tuple-element.35) | copy-start | bytes 589828
  369.3 45.3 %all-to-all-start.6 = ((bf16[16,3,64,192]{3,2,1,0:T(8,128)(2,1)}), bf16[16,3,64,192]{3,2,1,0:T(8,128)(2,1)S(1)}, u32[]{:S(2)}, u32[]{:S(2)}) async-start(bf16[16,3,64,192]{3,2,1,0:T(8,128)(2,1)} %pad_maximum_fusion), calls=%async_computation.6 | async-start | bytes 3145728 | tf_op jit(solution)/shard_map/all_to_all | solution.py:371
  376.6 49.6 %collective-permute-start.22 = (bf16[96,1792]{1,0:T(8,128)(2,1)S(1)}, bf16[96,1792]{1,0:T(8,128)(2,1)S(1)}, u32[]{:S(2)}, u32[]{:S(2)}) collective-permute-start(bf16[96,1792]{1,0:T(8,128)(2,1)S(1)} %bitcast.46), channel_id=1, source_target_pairs={{0,16},{16,0},{1,17},{17,1},{2,18},{18,2},{3,19},{19,3},{4,20},{20... | collective-permute-start | bytes 1032200 | tf_op jit(solution)/shard_map/ppermute | solution.py:367
Sparse Core Ops, SparseCore 0:
  11.1 90.8 all-gather.1
  228.5 62.0 reduce-scatter.1
